TPU v7x, 32 devices: a whole 2x2x4 slice. The times are simulated.
32 devices in a mesh: groups: 2 (over x), view: 16 (over z, y, core).
Axes of the slice: x: 2, y: 2, z: 4, core: 2. Of those that a mesh axis runs over, the one named last changes fastest.
Arguments:
- images: bfloat16 [32, 4, 32, 64, 256], P(('groups', 'view')), parts along dimension 0, may hold values from 0.5 to 2
- start_estimate: float32 [512, 64, 256], P(('groups', 'view')), parts along dimension 0, may hold values from 0.5 to 1.5
- view_order: int32 [4], replicated, may hold values from 0 to 3, each once
- psf_ranks: int32 [4], replicated, may hold values from 2 to 6, as said below
- depth_taps: float32 [4, 6, 17], replicated, may hold values from 0.05 to 1
- row_taps: float32 [4, 6, 17], replicated, may hold values from 0.05 to 1
- col_taps: float32 [4, 6, 17], replicated, may hold values from 0.05 to 1
- rank_weight: float32 [4, 6], replicated, may hold values from 0.1 to 1
Outputs:
- estimate: float32 [512, 64, 256], P(('groups', 'view')), parts along dimension 0
There are 2 independent parts, one for each index of `groups`. A program takes and returns all parts, laid end to end along the dimension named above; an argument that names none is the same for every part. Nothing has to cross between parts.
Inputs may be any that keep to these rules, and one draw needn't show every extreme that they name: `view_order`: each view appears exactly once. `psf_ranks`: some view uses 6 terms and some view uses 2.
All inputs are finite; a program needn't handle non-finite values.
Results may differ from a plain program's by a relative error of at most 0.0012.
Values sent between devices are 32-bit elements; how exact they have to be, the bound alone decides.
No kernel may reach another device: no remote copies, remote signals or barrier semaphores. Data moves between devices by JAX's collectives and lax.ppermute only.
A program may use at most 64 MiB of HBM per device.

v0:
```python
import jax
import jax.numpy as jnp
from jax import lax
from jax.sharding import PartitionSpec as P

TAPS = 17
STEPS = 4


def padded(cells, sides, width):
    for axis, dim in sides:
        count = lax.axis_size(axis)
        head = lax.slice_in_dim(cells, 0, width, axis=dim)
        tail = lax.slice_in_dim(cells, cells.shape[dim] - width, cells.shape[dim], axis=dim)
        cells = jnp.concatenate(
            [
                lax.ppermute(tail, axis, [(i, (i + 1) % count) for i in range(count)]),
                cells,
                lax.ppermute(head, axis, [((i + 1) % count, i) for i in range(count)]),
            ],
            axis=dim,
        )
    return cells


def shifted(shard, axis, by):
    devices = lax.axis_size(axis)
    return lax.ppermute(shard, axis, [(i, (i + by) % devices) for i in range(devices)])


def banded(taps, n_out, n_in, sign, offset):
    rows_out = jnp.arange(n_out, dtype=jnp.int32)[:, None]
    cols_in = jnp.arange(n_in, dtype=jnp.int32)[None, :]
    distance = sign * (cols_in - rows_out) + offset
    picks = (
        distance[:, :, None] == jnp.arange(taps.shape[-1], dtype=jnp.int32)[None, None, :]
    ).astype(jnp.float32)
    return jnp.einsum(
        "oik,rk->roi", picks, taps.astype(jnp.float32), precision=lax.Precision.HIGHEST
    ).astype(jnp.bfloat16)


def kernels(view_id, depth_taps, row_taps, col_taps, rank_weight, psf_ranks):
    live = (jnp.arange(depth_taps.shape[1], dtype=jnp.int32) < psf_ranks[view_id]).astype(
        jnp.float32
    )
    weights = rank_weight[view_id] * live
    weights = weights / jnp.sum(weights)
    depth_factor = (
        depth_taps[view_id] / jnp.sum(depth_taps[view_id], axis=1, keepdims=True) * weights[:, None]
    )
    row_factor = row_taps[view_id] / jnp.sum(row_taps[view_id], axis=1, keepdims=True)
    col_factor = col_taps[view_id] / jnp.sum(col_taps[view_id], axis=1, keepdims=True)
    return (
        depth_factor.astype(jnp.bfloat16),
        row_factor.astype(jnp.bfloat16),
        col_factor.astype(jnp.bfloat16),
    )


def operators(depth_factor, row_factor, col_factor, planes, row_count, col_count):
    margin = depth_factor.shape[1] // 2
    forward_depth = banded(depth_factor, planes + 2 * margin, planes + 4 * margin, 1, 0)
    forward_rows = banded(row_factor, row_count, row_count, 1, margin)
    forward_cols = banded(col_factor, col_count, col_count, 1, margin)
    adjoint_depth = banded(depth_factor, planes, planes + 2 * margin, -1, 2 * margin)
    adjoint_rows = banded(row_factor, row_count, row_count, -1, margin)
    adjoint_cols = banded(col_factor, col_count, col_count, -1, margin)
    return (forward_depth, forward_rows, forward_cols, adjoint_depth, adjoint_rows, adjoint_cols)


def refine(extended, observed, banded_ops):
    forward_depth, forward_rows, forward_cols, adjoint_depth, adjoint_rows, adjoint_cols = (
        banded_ops
    )
    single = jnp.float32
    half = jnp.bfloat16
    extended = extended.astype(half)
    partial_blur = jnp.einsum(
        "rqz,zyx->rqyx", forward_depth, extended, preferred_element_type=single
    ).astype(half)
    partial_blur = jnp.einsum(
        "ryv,rqvx->rqyx", forward_rows, partial_blur, preferred_element_type=single
    ).astype(half)
    blurred = jnp.einsum("rqyx,rwx->qyw", partial_blur, forward_cols, preferred_element_type=single)
    ratio = (observed / blurred).astype(half)
    partial_back = jnp.einsum(
        "rmq,qyx->rmyx", adjoint_depth, ratio, preferred_element_type=single
    ).astype(half)
    partial_back = jnp.einsum(
        "ryv,rmvx->rmyx", adjoint_rows, partial_back, preferred_element_type=single
    ).astype(half)
    return jnp.einsum("rmyx,rwx->myw", partial_back, adjoint_cols, preferred_element_type=single)


def shards(
    images, start_estimate, view_order, psf_ranks, depth_taps, row_taps, col_taps, rank_weight
):
    margin = TAPS // 2
    rim_width = 2 * margin
    loop_count = lax.axis_size("view")
    position = lax.axis_index("view")
    planes = start_estimate.shape[0]
    view_id = view_order[position % view_order.shape[0]]
    depth_factor, row_factor, col_factor = kernels(
        view_id, depth_taps, row_taps, col_taps, rank_weight, psf_ranks
    )
    banded_ops = operators(
        depth_factor,
        row_factor,
        col_factor,
        planes,
        start_estimate.shape[1],
        start_estimate.shape[2],
    )
    slabs = images[0]
    first_halo = padded(start_estimate, (("view", 0),), rim_width)
    below_start = first_halo[:rim_width]
    above_start = first_halo[-rim_width:]

    def update(own_block, below_planes, above_planes, step_index):
        block_index = (position - step_index) % loop_count
        below_live = (block_index > 0).astype(jnp.float32)
        above_live = (block_index < loop_count - 1).astype(jnp.float32)
        extended = jnp.concatenate(
            [below_planes * below_live, own_block, above_planes * above_live], axis=0
        )
        observed = lax.dynamic_index_in_dim(slabs, step_index, 0, keepdims=False)
        plane_ids = block_index * planes - margin + jnp.arange(planes + rim_width, dtype=jnp.int32)
        inside = (plane_ids >= 0) & (plane_ids < loop_count * planes)
        observed = jnp.where(
            inside[:, None, None], observed.astype(jnp.float32), jnp.zeros((), jnp.float32)
        )
        return own_block * refine(extended, observed, banded_ops)

    def advance(step_index, carry):
        own_block, below_planes, above_planes = carry
        updated = update(own_block, below_planes, above_planes, step_index)
        arrived = shifted(updated, "view", 1)
        below_next = shifted(updated, "view", 2)
        return (arrived, below_next, updated)

    final_block, below_end, above_end = lax.fori_loop(
        0, STEPS, advance, (start_estimate, below_start, above_start)
    )
    return shifted(final_block, "view", -STEPS)


def solution(mesh):
    in_specs = (
        P(("groups", "view"), None, None, None, None),
        P(("groups", "view"), None, None),
        P(),
        P(),
        P(),
        P(),
        P(),
        P(),
    )
    out_specs = P(("groups", "view"), None, None)
    return jax.shard_map(shards, mesh=mesh, in_specs=in_specs, out_specs=out_specs, check_vma=False)
```

profile of v0, /device:TPU:7, one launch (start us, length us, event | category | flops | bytes accessed | tf_op | source)
XLA Modules:
  0.0 305.5 jit_solution(10924421384826834958)
XLA Ops:
  0.0 1.8 copy.39
  1.8 1.9 collective-permute-start.2
  8.2 2.0 fusion.79
  10.2 2.0 broadcast_divide_fusion
  13.9 2.2 fusion.58
  16.2 2.3 fusion.57
  18.6 2.3 copy.42
  20.9 2.3 copy.45
  24.1 262.4 %while.19 = (s32[]{:T(128)}, f32[16,64,256]{2,0,1:T(8,128)S(1)}, f32[16,64,256]{2,0,1:T(8,128)S(1)}, f32[16,64,256]{2,0,1:T(8,128)}, s32[]{:T(128)}, /*index=5*/...) while((s32[]{:T(128)}, f32[16,64,256]{2,0,1:T(8,128)S(1)}, ...), condition=%wide.region_5.6_spmd, body=%wide.region_4.5_spmd.sunk | while | flops 3440378112 | bytes 54125088 | solution.py:143
  24.4 1.8 multiply_convert_fusion.3
  26.2 4.4 %convert_bitcast_fusion.4 = bf16[6,32,64,256]{3,1,0,2:T(8,128)(2,1)} fusion(bf16[16,64,256]{2,0,1:T(8,128)(2,1)S(1)} %get-tuple-element.451, bf16[16,64,256]{2,0,1:T(8,128)(2,1)S(1)} %convert.34, bf16[16,64,256]{2,0,1:T(8,128)(2,1)S(1)} %get-tuple-element.452, bf16[6,32,48]{2,1,0:T(8,128)(2,1)S(1)} %get-tuple-element.493), kind=kOutput, calls=%fused_computation.5.clone.1 | convolution fusion | flops 309854208 | bytes 7882752 | tf_op jit(solution)/shard_map/while/body/eval_jaxpr/rqz,zyx->rqyx/dot_general | solution.py:79
  30.6 10.7 %fusion.113 = bf16[32,64,256,1]{2,1,0,3:T(8,128)(2,1)} fusion(bf16[6,32,64,256]{3,1,0,2:T(8,128)(2,1)} %convert_bitcast_fusion.4, bf16[4,32,64,256]{3,2,1,0:T(8,128)(2,1)} %get-tuple-element.492, s32[]{:T(128)} %get-tuple-element.470, pred[32]{0:T(512)(128)(4,1)S(1)} %compare_and_fusion.2, bf16[6,256,256]{2,1,0:T(8,128)(2,1)S(1)} %copy-done.1, ...), kind=kOutput, calls=%fused_computation.20.clone.1 | convolution fusion | flops 2018508800 | bytes 9224228 | tf_op jit(solution)/shard_map/while/body/eval_jaxpr/rqyx,rwx->qyw/dot_general | solution.py:85
  41.3 2.2 convert_bitcast_fusion.5
  43.6 6.2 %fusion.114 = f32[16,64,256]{2,1,0:T(8,128)} fusion(bf16[6,16,64,256]{3,1,0,2:T(8,128)(2,1)S(1)} %convert_bitcast_fusion.5, f32[16,64,256]{2,0,1:T(8,128)} %copy-done, bf16[6,256,256]{2,1,0:T(8,128)(2,1)} %get-tuple-element.498, bf16[6,64,64]{2,1,0:T(8,128)(2,1)S(1)} %get-tuple-element.497), kind=kOutput, calls=%fused_computation.22.clone.1 | convolution fusion | flops 1008467968 | bytes 6078464 | tf_op jit(solution)/shard_map/while/body/eval_jaxpr/rmyx,rwx->myw/dot_general | solution.py:93
  49.8 2.6 collective-permute-start
  52.4 3.5 %collective-permute-start.1 = (f32[16,64,256]{2,1,0:T(8,128)}, f32[16,64,256]{2,1,0:T(8,128)}, u32[]{:S(2)}, u32[]{:S(2)}) collective-permute-start(f32[16,64,256]{2,1,0:T(8,128)} %fusion.114), channel_id=1, source_target_pairs={{0,2},{1,3},{2,4},{3,5},{4,6},{5,7},{6,8},{7,9},{8,10},{9,11},{10,... | collective-permute-start | bytes 3145736 | tf_op jit(solution)/shard_map/while/body/eval_jaxpr/ppermute | solution.py:28
  56.0 2.9 copy.131
  58.8 13.2 %collective-permute-done = f32[16,64,256]{2,1,0:T(8,128)S(1)} collective-permute-done((f32[16,64,256]{2,1,0:T(8,128)}, f32[16,64,256]{2,1,0:T(8,128)S(1)}, u32[]{:S(2)}, u32[]{:S(2)}) %collective-permute-start) | collective-permute-done | bytes 1048608 | tf_op jit(solution)/shard_map/while/body/eval_jaxpr/ppermute | solution.py:28
  72.6 17.4 %collective-permute-done.1 = f32[16,64,256]{2,1,0:T(8,128)} collective-permute-done((f32[16,64,256]{2,1,0:T(8,128)}, f32[16,64,256]{2,1,0:T(8,128)}, u32[]{:S(2)}, u32[]{:S(2)}) %collective-permute-start.1) | collective-permute-done | bytes 1048608 | tf_op jit(solution)/shard_map/while/body/eval_jaxpr/ppermute | solution.py:28
  90.0 1.8 copy.130
  92.0 1.8 multiply_convert_fusion.3
  93.8 4.4 %convert_bitcast_fusion.4 = bf16[6,32,64,256]{3,1,0,2:T(8,128)(2,1)} fusion(bf16[16,64,256]{2,0,1:T(8,128)(2,1)S(1)} %get-tuple-element.451, bf16[16,64,256]{2,0,1:T(8,128)(2,1)S(1)} %convert.34, bf16[16,64,256]{2,0,1:T(8,128)(2,1)S(1)} %get-tuple-element.452, bf16[6,32,48]{2,1,0:T(8,128)(2,1)S(1)} %get-tuple-element.493), kind=kOutput, calls=%fused_computation.5.clone.1 | convolution fusion | flops 309854208 | bytes 7882752 | tf_op jit(solution)/shard_map/while/body/eval_jaxpr/rqz,zyx->rqyx/dot_general | solution.py:79
  98.2 10.7 %fusion.113 = bf16[32,64,256,1]{2,1,0,3:T(8,128)(2,1)} fusion(bf16[6,32,64,256]{3,1,0,2:T(8,128)(2,1)} %convert_bitcast_fusion.4, bf16[4,32,64,256]{3,2,1,0:T(8,128)(2,1)} %get-tuple-element.492, s32[]{:T(128)} %get-tuple-element.470, pred[32]{0:T(512)(128)(4,1)S(1)} %compare_and_fusion.2, bf16[6,256,256]{2,1,0:T(8,128)(2,1)S(1)} %copy-done.1, ...), kind=kOutput, calls=%fused_computation.20.clone.1 | convolution fusion | flops 2018508800 | bytes 9224228 | tf_op jit(solution)/shard_map/while/body/eval_jaxpr/rqyx,rwx->qyw/dot_general | solution.py:85
  108.9 2.2 convert_bitcast_fusion.5
  111.1 6.2 %fusion.114 = f32[16,64,256]{2,1,0:T(8,128)} fusion(bf16[6,16,64,256]{3,1,0,2:T(8,128)(2,1)S(1)} %convert_bitcast_fusion.5, f32[16,64,256]{2,0,1:T(8,128)} %copy-done, bf16[6,256,256]{2,1,0:T(8,128)(2,1)} %get-tuple-element.498, bf16[6,64,64]{2,1,0:T(8,128)(2,1)S(1)} %get-tuple-element.497), kind=kOutput, calls=%fused_computation.22.clone.1 | convolution fusion | flops 1008467968 | bytes 6078464 | tf_op jit(solution)/shard_map/while/body/eval_jaxpr/rmyx,rwx->myw/dot_general | solution.py:93
  117.9 2.9 copy.131
  120.7 18.4 %collective-permute-done = f32[16,64,256]{2,1,0:T(8,128)S(1)} collective-permute-done((f32[16,64,256]{2,1,0:T(8,128)}, f32[16,64,256]{2,1,0:T(8,128)S(1)}, u32[]{:S(2)}, u32[]{:S(2)}) %collective-permute-start) | collective-permute-done | bytes 1048608 | tf_op jit(solution)/shard_map/while/body/eval_jaxpr/ppermute | solution.py:28
  139.8 15.0 %collective-permute-done.1 = f32[16,64,256]{2,1,0:T(8,128)} collective-permute-done((f32[16,64,256]{2,1,0:T(8,128)}, f32[16,64,256]{2,1,0:T(8,128)}, u32[]{:S(2)}, u32[]{:S(2)}) %collective-permute-start.1) | collective-permute-done | bytes 1048608 | tf_op jit(solution)/shard_map/while/body/eval_jaxpr/ppermute | solution.py:28
  154.7 1.8 copy.130
  156.7 1.8 multiply_convert_fusion.3
  158.5 4.4 %convert_bitcast_fusion.4 = bf16[6,32,64,256]{3,1,0,2:T(8,128)(2,1)} fusion(bf16[16,64,256]{2,0,1:T(8,128)(2,1)S(1)} %get-tuple-element.451, bf16[16,64,256]{2,0,1:T(8,128)(2,1)S(1)} %convert.34, bf16[16,64,256]{2,0,1:T(8,128)(2,1)S(1)} %get-tuple-element.452, bf16[6,32,48]{2,1,0:T(8,128)(2,1)S(1)} %get-tuple-element.493), kind=kOutput, calls=%fused_computation.5.clone.1 | convolution fusion | flops 309854208 | bytes 7882752 | tf_op jit(solution)/shard_map/while/body/eval_jaxpr/rqz,zyx->rqyx/dot_general | solution.py:79
  162.9 10.7 %fusion.113 = bf16[32,64,256,1]{2,1,0,3:T(8,128)(2,1)} fusion(bf16[6,32,64,256]{3,1,0,2:T(8,128)(2,1)} %convert_bitcast_fusion.4, bf16[4,32,64,256]{3,2,1,0:T(8,128)(2,1)} %get-tuple-element.492, s32[]{:T(128)} %get-tuple-element.470, pred[32]{0:T(512)(128)(4,1)S(1)} %compare_and_fusion.2, bf16[6,256,256]{2,1,0:T(8,128)(2,1)S(1)} %copy-done.1, ...), kind=kOutput, calls=%fused_computation.20.clone.1 | convolution fusion | flops 2018508800 | bytes 9224228 | tf_op jit(solution)/shard_map/while/body/eval_jaxpr/rqyx,rwx->qyw/dot_general | solution.py:85
  173.7 2.2 convert_bitcast_fusion.5
  175.9 6.2 %fusion.114 = f32[16,64,256]{2,1,0:T(8,128)} fusion(bf16[6,16,64,256]{3,1,0,2:T(8,128)(2,1)S(1)} %convert_bitcast_fusion.5, f32[16,64,256]{2,0,1:T(8,128)} %copy-done, bf16[6,256,256]{2,1,0:T(8,128)(2,1)} %get-tuple-element.498, bf16[6,64,64]{2,1,0:T(8,128)(2,1)S(1)} %get-tuple-element.497), kind=kOutput, calls=%fused_computation.22.clone.1 | convolution fusion | flops 1008467968 | bytes 6078464 | tf_op jit(solution)/shard_map/while/body/eval_jaxpr/rmyx,rwx->myw/dot_general | solution.py:93
  182.1 2.9 copy.131
  185.0 19.5 %collective-permute-done = f32[16,64,256]{2,1,0:T(8,128)S(1)} collective-permute-done((f32[16,64,256]{2,1,0:T(8,128)}, f32[16,64,256]{2,1,0:T(8,128)S(1)}, u32[]{:S(2)}, u32[]{:S(2)}) %collective-permute-start) | collective-permute-done | bytes 1048608 | tf_op jit(solution)/shard_map/while/body/eval_jaxpr/ppermute | solution.py:28
  205.1 14.0 %collective-permute-done.1 = f32[16,64,256]{2,1,0:T(8,128)} collective-permute-done((f32[16,64,256]{2,1,0:T(8,128)}, f32[16,64,256]{2,1,0:T(8,128)}, u32[]{:S(2)}, u32[]{:S(2)}) %collective-permute-start.1) | collective-permute-done | bytes 1048608 | tf_op jit(solution)/shard_map/while/body/eval_jaxpr/ppermute | solution.py:28
  219.1 1.8 copy.130
  221.1 1.8 multiply_convert_fusion.3
  222.9 4.4 %convert_bitcast_fusion.4 = bf16[6,32,64,256]{3,1,0,2:T(8,128)(2,1)} fusion(bf16[16,64,256]{2,0,1:T(8,128)(2,1)S(1)} %get-tuple-element.451, bf16[16,64,256]{2,0,1:T(8,128)(2,1)S(1)} %convert.34, bf16[16,64,256]{2,0,1:T(8,128)(2,1)S(1)} %get-tuple-element.452, bf16[6,32,48]{2,1,0:T(8,128)(2,1)S(1)} %get-tuple-element.493), kind=kOutput, calls=%fused_computation.5.clone.1 | convolution fusion | flops 309854208 | bytes 7882752 | tf_op jit(solution)/shard_map/while/body/eval_jaxpr/rqz,zyx->rqyx/dot_general | solution.py:79
  227.3 10.7 %fusion.113 = bf16[32,64,256,1]{2,1,0,3:T(8,128)(2,1)} fusion(bf16[6,32,64,256]{3,1,0,2:T(8,128)(2,1)} %convert_bitcast_fusion.4, bf16[4,32,64,256]{3,2,1,0:T(8,128)(2,1)} %get-tuple-element.492, s32[]{:T(128)} %get-tuple-element.470, pred[32]{0:T(512)(128)(4,1)S(1)} %compare_and_fusion.2, bf16[6,256,256]{2,1,0:T(8,128)(2,1)S(1)} %copy-done.1, ...), kind=kOutput, calls=%fused_computation.20.clone.1 | convolution fusion | flops 2018508800 | bytes 9224228 | tf_op jit(solution)/shard_map/while/body/eval_jaxpr/rqyx,rwx->qyw/dot_general | solution.py:85
  238.1 2.2 convert_bitcast_fusion.5
  240.3 6.2 %fusion.114 = f32[16,64,256]{2,1,0:T(8,128)} fusion(bf16[6,16,64,256]{3,1,0,2:T(8,128)(2,1)S(1)} %convert_bitcast_fusion.5, f32[16,64,256]{2,0,1:T(8,128)} %copy-done, bf16[6,256,256]{2,1,0:T(8,128)(2,1)} %get-tuple-element.498, bf16[6,64,64]{2,1,0:T(8,128)(2,1)S(1)} %get-tuple-element.497), kind=kOutput, calls=%fused_computation.22.clone.1 | convolution fusion | flops 1008467968 | bytes 6078464 | tf_op jit(solution)/shard_map/while/body/eval_jaxpr/rmyx,rwx->myw/dot_general | solution.py:93
  246.9 2.9 copy.131
  249.7 18.7 %collective-permute-done = f32[16,64,256]{2,1,0:T(8,128)S(1)} collective-permute-done((f32[16,64,256]{2,1,0:T(8,128)}, f32[16,64,256]{2,1,0:T(8,128)S(1)}, u32[]{:S(2)}, u32[]{:S(2)}) %collective-permute-start) | collective-permute-done | bytes 1048608 | tf_op jit(solution)/shard_map/while/body/eval_jaxpr/ppermute | solution.py:28
  269.1 15.6 %collective-permute-done.1 = f32[16,64,256]{2,1,0:T(8,128)} collective-permute-done((f32[16,64,256]{2,1,0:T(8,128)}, f32[16,64,256]{2,1,0:T(8,128)}, u32[]{:S(2)}, u32[]{:S(2)}) %collective-permute-start.1) | collective-permute-done | bytes 1048608 | tf_op jit(solution)/shard_map/while/body/eval_jaxpr/ppermute | solution.py:28
  284.6 1.8 copy.130
  287.5 17.0 %collective-permute-done.4 = f32[16,64,256]{2,1,0:T(8,128)S(1)} collective-permute-done((f32[16,64,256]{2,1,0:T(8,128)S(1)}, f32[16,64,256]{2,1,0:T(8,128)S(1)}, u32[]{:S(2)}, u32[]{:S(2)}) %collective-permute-start.4) | collective-permute-done | bytes 1048608 | tf_op jit(solution)/shard_map/ppermute | solution.py:28
  (58 shorter events, 10.8 us)
Async XLA Ops:
  1.8 22.2 %collective-permute-start.2 = (f32[16,64,256]{2,0,1:T(8,128)S(1)}, f32[16,64,256]{2,0,1:T(8,128)S(1)}, u32[]{:S(2)}, u32[]{:S(2)}) collective-permute-start(f32[16,64,256]{2,0,1:T(8,128)S(1)} %copy.39), channel_id=1, source_target_pairs={{0,1},{1,2},{2,3},{3,4},{4,5},{5,6},{6,7},{7,8},{8,9},{9,10},{10,1... | collective-permute-start | bytes 3145736 | tf_op jit(solution)/shard_map/ppermute | solution.py:17
  3.7 20.4 %collective-permute-start.3 = (f32[16,64,256]{2,0,1:T(8,128)S(1)}, f32[16,64,256]{2,0,1:T(8,128)}, u32[]{:S(2)}, u32[]{:S(2)}) collective-permute-start(f32[16,64,256]{2,0,1:T(8,128)S(1)} %copy.39), channel_id=1, source_target_pairs={{1,0},{2,1},{3,2},{4,3},{5,4},{6,5},{7,6},{8,7},{9,8},{10,9},{11,1... | collective-permute-start | bytes 3145736 | tf_op jit(solution)/shard_map/ppermute | solution.py:19
  24.3 6.3 %copy-start = (f32[16,64,256]{2,0,1:T(8,128)}, f32[16,64,256]{2,0,1:T(8,128)S(1)}, u32[]{:S(2)}) copy-start(f32[16,64,256]{2,0,1:T(8,128)S(1)} %get-tuple-element.471) | copy-start | bytes 3145732 | tf_op jit(solution)/shard_map/while
  26.2 4.4 %copy-start.1 = (bf16[6,256,256]{2,1,0:T(8,128)(2,1)S(1)}, bf16[6,256,256]{2,1,0:T(8,128)(2,1)}, u32[]{:S(2)}) copy-start(bf16[6,256,256]{2,1,0:T(8,128)(2,1)} %get-tuple-element.495) | copy-start | bytes 2359300 | tf_op jit(solution)/shard_map/while
  49.8 22.2 %collective-permute-start = (f32[16,64,256]{2,1,0:T(8,128)}, f32[16,64,256]{2,1,0:T(8,128)S(1)}, u32[]{:S(2)}, u32[]{:S(2)}) collective-permute-start(f32[16,64,256]{2,1,0:T(8,128)} %fusion.114), channel_id=1, source_target_pairs={{0,1},{1,2},{2,3},{3,4},{4,5},{5,6},{6,7},{7,8},{8,9},{9,10},{10,1... | collective-permute-start | bytes 3145736 | tf_op jit(solution)/shard_map/while/body/eval_jaxpr/ppermute | solution.py:28
  52.4 37.6 %collective-permute-start.1 = (f32[16,64,256]{2,1,0:T(8,128)}, f32[16,64,256]{2,1,0:T(8,128)}, u32[]{:S(2)}, u32[]{:S(2)}) collective-permute-start(f32[16,64,256]{2,1,0:T(8,128)} %fusion.114), channel_id=1, source_target_pairs={{0,2},{1,3},{2,4},{3,5},{4,6},{5,7},{6,8},{7,9},{8,10},{9,11},{10,... | collective-permute-start | bytes 3145736 | tf_op jit(solution)/shard_map/while/body/eval_jaxpr/ppermute | solution.py:28
  91.9 6.3 %copy-start = (f32[16,64,256]{2,0,1:T(8,128)}, f32[16,64,256]{2,0,1:T(8,128)S(1)}, u32[]{:S(2)}) copy-start(f32[16,64,256]{2,0,1:T(8,128)S(1)} %get-tuple-element.471) | copy-start | bytes 3145732 | tf_op jit(solution)/shard_map/while
  93.8 4.4 %copy-start.1 = (bf16[6,256,256]{2,1,0:T(8,128)(2,1)S(1)}, bf16[6,256,256]{2,1,0:T(8,128)(2,1)}, u32[]{:S(2)}) copy-start(bf16[6,256,256]{2,1,0:T(8,128)(2,1)} %get-tuple-element.495) | copy-start | bytes 2359300 | tf_op jit(solution)/shard_map/while
  117.4 21.8 %collective-permute-start = (f32[16,64,256]{2,1,0:T(8,128)}, f32[16,64,256]{2,1,0:T(8,128)S(1)}, u32[]{:S(2)}, u32[]{:S(2)}) collective-permute-start(f32[16,64,256]{2,1,0:T(8,128)} %fusion.114), channel_id=1, source_target_pairs={{0,1},{1,2},{2,3},{3,4},{4,5},{5,6},{6,7},{7,8},{8,9},{9,10},{10,1... | collective-permute-start | bytes 3145736 | tf_op jit(solution)/shard_map/while/body/eval_jaxpr/ppermute | solution.py:28
  117.4 37.4 %collective-permute-start.1 = (f32[16,64,256]{2,1,0:T(8,128)}, f32[16,64,256]{2,1,0:T(8,128)}, u32[]{:S(2)}, u32[]{:S(2)}) collective-permute-start(f32[16,64,256]{2,1,0:T(8,128)} %fusion.114), channel_id=1, source_target_pairs={{0,2},{1,3},{2,4},{3,5},{4,6},{5,7},{6,8},{7,9},{8,10},{9,11},{10,... | collective-permute-start | bytes 3145736 | tf_op jit(solution)/shard_map/while/body/eval_jaxpr/ppermute | solution.py:28
  156.6 6.3 %copy-start = (f32[16,64,256]{2,0,1:T(8,128)}, f32[16,64,256]{2,0,1:T(8,128)S(1)}, u32[]{:S(2)}) copy-start(f32[16,64,256]{2,0,1:T(8,128)S(1)} %get-tuple-element.471) | copy-start | bytes 3145732 | tf_op jit(solution)/shard_map/while
  158.5 4.4 %copy-start.1 = (bf16[6,256,256]{2,1,0:T(8,128)(2,1)S(1)}, bf16[6,256,256]{2,1,0:T(8,128)(2,1)}, u32[]{:S(2)}) copy-start(bf16[6,256,256]{2,1,0:T(8,128)(2,1)} %get-tuple-element.495) | copy-start | bytes 2359300 | tf_op jit(solution)/shard_map/while
  182.1 22.3 %collective-permute-start = (f32[16,64,256]{2,1,0:T(8,128)}, f32[16,64,256]{2,1,0:T(8,128)S(1)}, u32[]{:S(2)}, u32[]{:S(2)}) collective-permute-start(f32[16,64,256]{2,1,0:T(8,128)} %fusion.114), channel_id=1, source_target_pairs={{0,1},{1,2},{2,3},{3,4},{4,5},{5,6},{6,7},{7,8},{8,9},{9,10},{10,1... | collective-permute-start | bytes 3145736 | tf_op jit(solution)/shard_map/while/body/eval_jaxpr/ppermute | solution.py:28
  182.1 37.0 %collective-permute-start.1 = (f32[16,64,256]{2,1,0:T(8,128)}, f32[16,64,256]{2,1,0:T(8,128)}, u32[]{:S(2)}, u32[]{:S(2)}) collective-permute-start(f32[16,64,256]{2,1,0:T(8,128)} %fusion.114), channel_id=1, source_target_pairs={{0,2},{1,3},{2,4},{3,5},{4,6},{5,7},{6,8},{7,9},{8,10},{9,11},{10,... | collective-permute-start | bytes 3145736 | tf_op jit(solution)/shard_map/while/body/eval_jaxpr/ppermute | solution.py:28
  221.0 6.3 %copy-start = (f32[16,64,256]{2,0,1:T(8,128)}, f32[16,64,256]{2,0,1:T(8,128)S(1)}, u32[]{:S(2)}) copy-start(f32[16,64,256]{2,0,1:T(8,128)S(1)} %get-tuple-element.471) | copy-start | bytes 3145732 | tf_op jit(solution)/shard_map/while
  222.9 4.4 %copy-start.1 = (bf16[6,256,256]{2,1,0:T(8,128)(2,1)S(1)}, bf16[6,256,256]{2,1,0:T(8,128)(2,1)}, u32[]{:S(2)}) copy-start(bf16[6,256,256]{2,1,0:T(8,128)(2,1)} %get-tuple-element.495) | copy-start | bytes 2359300 | tf_op jit(solution)/shard_map/while
  246.5 21.9 %collective-permute-start = (f32[16,64,256]{2,1,0:T(8,128)}, f32[16,64,256]{2,1,0:T(8,128)S(1)}, u32[]{:S(2)}, u32[]{:S(2)}) collective-permute-start(f32[16,64,256]{2,1,0:T(8,128)} %fusion.114), channel_id=1, source_target_pairs={{0,1},{1,2},{2,3},{3,4},{4,5},{5,6},{6,7},{7,8},{8,9},{9,10},{10,1... | collective-permute-start | bytes 3145736 | tf_op jit(solution)/shard_map/while/body/eval_jaxpr/ppermute | solution.py:28
  246.5 38.1 %collective-permute-start.1 = (f32[16,64,256]{2,1,0:T(8,128)}, f32[16,64,256]{2,1,0:T(8,128)}, u32[]{:S(2)}, u32[]{:S(2)}) collective-permute-start(f32[16,64,256]{2,1,0:T(8,128)} %fusion.114), channel_id=1, source_target_pairs={{0,2},{1,3},{2,4},{3,5},{4,6},{5,7},{6,8},{7,9},{8,10},{9,11},{10,... | collective-permute-start | bytes 3145736 | tf_op jit(solution)/shard_map/while/body/eval_jaxpr/ppermute | solution.py:28
  287.1 17.5 %collective-permute-start.4 = (f32[16,64,256]{2,1,0:T(8,128)S(1)}, f32[16,64,256]{2,1,0:T(8,128)S(1)}, u32[]{:S(2)}, u32[]{:S(2)}) collective-permute-start(f32[16,64,256]{2,1,0:T(8,128)S(1)} %copy.46), channel_id=1, source_target_pairs={{0,12},{1,13},{2,14},{3,15},{4,0},{5,1},{6,2},{7,3},{8,4},{9,5},{1... | collective-permute-start | bytes 3145736 | tf_op jit(solution)/shard_map/ppermute | solution.py:28
where the time goes:
time: 307 us; the launch traced here: 306 us
  waiting for transfers between devices  149 us (49%)
  matrix products  99.8 us (33%)
  local copies, waits for them, and re-layouts  31.8 us (10%)
  other arithmetic  13.2 us (4%)
  starting transfers between devices  9.26 us (3%)
    ppermute x9, waiting for transfers between devices, shifted(): lax.ppermute(shard, axis, [(i, (i + by) % devices) for i in range(devices)])  149 us
    dot_general x4, matrix products, refine(): jnp.einsum('rqyx,rwx->qyw', partial_blur, forward_cols, preferred_element...  42.9 us
    dot_general x4, matrix products, refine(): jnp.einsum('rmyx,rwx->myw', partial_back, adjoint_cols, preferred_element...  25 us
    another operation x12, local copies, waits for them, and re-layouts  21.2 us
    dot_general x4, matrix products, refine(): jnp.einsum('rqz,zyx->rqyx', forward_depth, extended, preferred_element_ty...  17.7 us
    dot_general x4, matrix products, refine(): jnp.einsum('rmq,qyx->rmyx', adjoint_depth, ratio, preferred_element_type=...  8.85 us
    ppermute x9, starting transfers between devices, shifted(): lax.ppermute(shard, axis, [(i, (i + by) % devices) for i in range(devices)])  7.41 us
    another operation x8, other arithmetic  7.31 us
  transfers between devices with their start and end apart: 11, of which 9 were waited for; matrix products, arithmetic and copies ran while one was open for 11% of the time, Pallas kernels for 0%

commit v1 on v0

v1 whole, which is shorter than its diff:
```python
import jax
import jax.numpy as jnp
from jax import lax
from jax.experimental import pallas as pl
from jax.experimental.pallas import tpu as pltpu
from jax.sharding import PartitionSpec as P

STEPS = 4
ROW_GROUP = 8
PLANE_GROUP = 4

F32 = jnp.float32
BF16 = jnp.bfloat16


def dot(a, b):
    return jnp.dot(a, b, preferred_element_type=F32)


def factors(view_id, depth_taps, row_taps, col_taps, rank_weight, psf_ranks):
    live = (jnp.arange(depth_taps.shape[1], dtype=jnp.int32) < psf_ranks[view_id]).astype(F32)
    weights = rank_weight[view_id] * live
    weights = weights / jnp.sum(weights)
    depth = depth_taps[view_id]
    row = row_taps[view_id]
    col = col_taps[view_id]
    depth = depth / jnp.sum(depth, axis=1, keepdims=True) * weights[:, None]
    row = row / jnp.sum(row, axis=1, keepdims=True)
    col = col / jnp.sum(col, axis=1, keepdims=True)
    return jnp.stack([depth, row, col])


def build_kernel(taps, depth_f, depth_a, row_f, row_a, col_f, col_a):
    ranks = depth_f.shape[0]
    count = taps.shape[2]
    margin = count // 2

    def toeplitz(kind, r, dist, scale):
        total = jnp.zeros(dist.shape, F32)
        for k in range(count):
            total = jnp.where(dist == scale * k, taps[kind, r, k], total)
        return total

    def diff(n, m):
        return lax.broadcasted_iota(jnp.int32, (n, m), 1) - lax.broadcasted_iota(
            jnp.int32, (n, m), 0
        )

    def one(r, carry):
        d = diff(depth_f.shape[1], depth_f.shape[2])
        depth_f[r] = toeplitz(0, r, d, ROW_GROUP).astype(BF16)
        depth_a[r] = toeplitz(0, r, ROW_GROUP * (count - 1) - d, ROW_GROUP).astype(BF16)
        n = col_f.shape[1]
        d = diff(n, n)
        col_a[r] = toeplitz(2, r, d + margin, 1).astype(BF16)
        col_f[r] = toeplitz(2, r, margin - d, 1).astype(BF16)
        n = row_f.shape[1]
        d = diff(n, n)
        rows = n // PLANE_GROUP
        same = lax.broadcasted_iota(jnp.int32, (n, n), 0) // rows == (
            lax.broadcasted_iota(jnp.int32, (n, n), 1) // rows
        )
        d = jnp.where(same, d, n)
        row_f[r] = toeplitz(1, r, d + margin, 1).astype(BF16)
        row_a[r] = toeplitz(1, r, margin - d, 1).astype(BF16)
        return carry

    lax.fori_loop(0, ranks, one, 0)


def build(taps, planes, rows, cols):
    ranks = taps.shape[1]
    depth = jax.ShapeDtypeStruct((ranks, planes * ROW_GROUP, 2 * planes * ROW_GROUP), BF16)
    row = jax.ShapeDtypeStruct((ranks, PLANE_GROUP * rows, PLANE_GROUP * rows), BF16)
    col = jax.ShapeDtypeStruct((ranks, cols, cols), BF16)
    return pl.pallas_call(
        build_kernel,
        out_shape=[depth, depth, row, row, col, col],
        in_specs=[pl.BlockSpec(memory_space=pltpu.SMEM)],
        out_specs=[pl.BlockSpec(memory_space=pltpu.VMEM)] * 6,
        compiler_params=pltpu.CompilerParams(vmem_limit_bytes=24 * 2**20),
        name="build",
    )(taps)


def depth_pass(first, second, op, out, start, scale=None):
    ranks = op.shape[0]
    planes, rows, cols = first.shape
    step = 2 * ROW_GROUP

    def one(i, carry):
        tiles = []
        for half in range(2):
            y = pl.ds(pl.multiple_of(i * step + half * ROW_GROUP, ROW_GROUP), ROW_GROUP)
            tail = second[:, y, :] if scale is None else second[:, y, :] * scale
            both = jnp.concatenate([first[:, y, :], tail], axis=0)
            tiles.append(both.reshape(2 * planes * ROW_GROUP, cols).astype(BF16))
        y = pl.ds(pl.multiple_of(i * step, step), step)
        for r in range(ranks):
            parts = [dot(op[r], tile).reshape(planes, ROW_GROUP, cols) for tile in tiles]
            out[r, pl.ds(start, planes), y, :] = jnp.concatenate(parts, axis=1).astype(BF16)
        return carry

    lax.fori_loop(0, rows // step, one, 0)


def row_pass(src, op, out, planes):
    ranks, _, rows, cols = src.shape
    size = PLANE_GROUP * rows

    def one(i, carry):
        at = pl.multiple_of(i * size, size)
        for r in range(ranks):
            data = src[r, pl.ds(i * PLANE_GROUP, PLANE_GROUP)].reshape(size, cols)
            out[pl.ds(at, size), r * cols : (r + 1) * cols] = dot(op[r], data).astype(BF16)
        return carry

    lax.fori_loop(0, planes // PLANE_GROUP, one, 0)


def col_pass(src, op, planes, rows, finish):
    ranks, cols, _ = op.shape
    size = PLANE_GROUP * rows
    weights = op[...].reshape(ranks * cols, cols)

    def one(i, carry):
        at = pl.multiple_of(i * size, size)
        result = dot(src[pl.ds(at, size), :], weights)
        finish(i * PLANE_GROUP, result.reshape(PLANE_GROUP, rows, cols))
        return carry

    lax.fori_loop(0, planes // PLANE_GROUP, one, 0)


def step_kernel(
    step,
    margin,
    block,
    below,
    own,
    above,
    images,
    depth_f,
    depth_a,
    row_f,
    row_a,
    col_f,
    col_a,
    out,
    spread,
    mixed,
    ratio,
    observed,
    sem,
):
    planes, rows, cols = own.shape
    slab = observed.shape[0]
    copy = pltpu.make_async_copy(images.at[0, step], observed, sem)
    copy.start()

    depth_pass(below, own, depth_f, spread, 0)
    depth_pass(own, above, depth_f, spread, planes, block[1].astype(F32))
    row_pass(spread, row_f, mixed, slab)
    copy.wait()

    def to_ratio(q, blurred):
        z = lax.broadcasted_iota(jnp.int32, (PLANE_GROUP, 1, 1), 0) + (
            q + block[0] * planes - margin
        )
        inside = (z >= 0) & (z < block[2] * planes)
        seen = observed[pl.ds(q, PLANE_GROUP)].astype(F32)
        value = jnp.where(inside, seen, 0.0) / blurred
        ratio[pl.ds(q, PLANE_GROUP)] = value

    col_pass(mixed, col_f, slab, rows, to_ratio)
    depth_pass(ratio.at[pl.ds(0, planes)], ratio.at[pl.ds(planes, planes)], depth_a, spread, 0)
    row_pass(spread, row_a, mixed, planes)

    def to_update(m, back):
        at = pl.ds(m, PLANE_GROUP)
        out[at] = own[at] * back

    col_pass(mixed, col_a, planes, rows, to_update)


def refine(step, margin, block, below, own, above, images, ops):
    planes, rows, cols = own.shape
    ranks = ops[0].shape[0]
    slab = images.shape[2]
    vmem = pl.BlockSpec(memory_space=pltpu.VMEM)

    def kernel(*refs):
        step_kernel(step, margin, *refs)

    return pl.pallas_call(
        kernel,
        out_shape=jax.ShapeDtypeStruct(own.shape, F32),
        in_specs=[pl.BlockSpec(memory_space=pltpu.SMEM)]
        + [vmem] * 3
        + [pl.BlockSpec(memory_space=pl.ANY)]
        + [vmem] * 6,
        out_specs=vmem,
        scratch_shapes=[
            pltpu.VMEM((ranks, slab, rows, cols), BF16),
            pltpu.VMEM((slab * rows, ranks * cols), BF16),
            pltpu.VMEM((slab, rows, cols), F32),
            pltpu.VMEM((slab, rows, cols), BF16),
            pltpu.SemaphoreType.DMA,
        ],
        compiler_params=pltpu.CompilerParams(vmem_limit_bytes=44 * 2**20),
        name="refine",
    )(block, below, own, above, images, *ops)


def shards(
    images, start_estimate, view_order, psf_ranks, depth_taps, row_taps, col_taps, rank_weight
):
    margin = depth_taps.shape[2] // 2
    count = lax.axis_size("view")
    position = lax.axis_index("view")
    planes, rows, cols = start_estimate.shape

    def send(cells, by, skip=()):
        pairs = [(i, (i + by) % count) for i in range(count) if i not in skip]
        return lax.ppermute(cells, "view", pairs)

    own = start_estimate
    below = send(own, 1, (count - 1,))
    above = send(own, -1, (0,))

    view_id = view_order[position % view_order.shape[0]]
    taps = factors(view_id, depth_taps, row_taps, col_taps, rank_weight, psf_ranks)
    ops = build(taps.astype(BF16).astype(F32), planes, rows, cols)

    for step in range(STEPS):
        block = (position - step) % count
        facts = jnp.stack(
            [block, (block < count - 1).astype(jnp.int32), jnp.int32(count)]
        ).astype(jnp.int32)
        updated = refine(step, margin, facts, below, own, above, images, ops)
        if step < STEPS - 1:
            own = send(updated, 1)
            below = send(own, 1, (step,))
            above = updated
    return send(updated, -(STEPS - 1))


def solution(mesh):
    in_specs = (
        P(("groups", "view"), None, None, None, None),
        P(("groups", "view"), None, None),
        P(),
        P(),
        P(),
        P(),
        P(),
        P(),
    )
    out_specs = P(("groups", "view"), None, None)
    return jax.shard_map(shards, mesh=mesh, in_specs=in_specs, out_specs=out_specs, check_vma=False)
```

time: 307 us -> 220 us (0.72)
  the two profiles are of different devices: /device:TPU:7 before, /device:TPU:0 now
where the time goes in v1:
time: 220 us; the launch traced here: 219 us
  waiting for transfers between devices  111 us (50%)
  Pallas kernels  68.3 us (31%)
  local copies, waits for them, and re-layouts  16 us (7%)
  starting transfers between devices  15.5 us (7%)
  other arithmetic  6.02 us (3%)
    ppermute x9, waiting for transfers between devices, send(): return lax.ppermute(cells, 'view', pairs)  111 us
    pallas_call x4, Pallas kernels, refine(): pl.pallas_call(kernel, out_shape=jax.ShapeDtypeStruct(own.shape, F32), in...  61.3 us
    ppermute x9, starting transfers between devices, send(): return lax.ppermute(cells, 'view', pairs)  15.5 us
    unnamed x25, local copies, waits for them, and re-layouts  13.5 us
    pallas_call x1, Pallas kernels, build(): pl.pallas_call(build_kernel, out_shape=[depth, depth, row, row, col, col]...  7.06 us
  transfers between devices with their start and end apart: 9, of which 7 were waited for; matrix products, arithmetic and copies ran while one was open for 4% of the time, Pallas kernels for 3%

profile of v1, /device:TPU:0, one launch (start us, length us, event | category | flops | bytes accessed | tf_op | source)
XLA Modules:
  0.0 219.2 jit_solution(9824372115679666703)
XLA Ops:
  0.0 3.3 %collective-permute-start = (f32[16,64,256]{2,1,0:T(8,128)}, f32[16,64,256]{2,1,0:T(8,128)}, u32[]{:S(2)}, u32[]{:S(2)}) collective-permute-start(f32[16,64,256]{2,1,0:T(8,128)} %refs_2_.1), channel_id=1, source_target_pairs={{0,1},{1,2},{2,3},{3,4},{4,5},{5,6},{6,7},{7,8},{8,9},{9,10},{10,1... | collective-permute-start | bytes 3145736 | tf_op jit(solution)/shard_map/ppermute | solution.py:225
  3.3 1.3 collective-permute-start.1
  4.6 1.2 dynamic_slice.18
  7.8 1.2 dynamic_slice.20
  9.1 0.8 fusion.8
  9.9 1.9 fusion.5
  11.8 1.9 broadcast_divide_fusion
  13.7 0.9 fusion.6
  14.6 0.1 fusion.1
  14.6 0.1 fusion
  14.7 0.1 fusion.3
  14.8 7.1 %build.1 = (bf16[6,128,256]{2,1,0:T(8,128)(2,1)S(1)}, bf16[6,128,256]{2,1,0:T(8,128)(2,1)S(1)}, bf16[6,256,256]{2,1,0:T(8,128)(2,1)S(1)}, bf16[6,256,256]{2,1,0:...) custom-call(f32[3,6,17]{2,1,0:T(8,128)S(1)} %maximum_convert_fusion.taps), custom_call_target="tpu_custom_call" | custom-call | tf_op jit(solution)/shard_map/build/pallas_call | solution.py:76
  21.9 0.7 copy-done
  22.6 0.1 pad_add_fusion.refs_0_
  22.7 1.0 copy-done.1
  23.7 1.2 copy-done.11
  24.9 15.3 %refine.4.refs_3_ = f32[16,64,256]{2,1,0:T(8,128)S(1)} custom-call(s32[3]{0:T(128)S(1)} %pad_add_fusion.refs_0_, f32[16,64,256]{2,1,0:T(8,128)} %collective-permute-done.refs_1_, f32[16,64,256]{2,1,0:T(8,128)S(1)} %copy-done.11, f32[16,64,256]{2,1,0:T(8,128)} %collective-permute-done.1.refs_3_, bf16[1,4,32,64,256]{4,3,2,1,0:T(8,128)(2,1)} %refs_4_.7, ...), custom_call_target="tpu_custom_call" | custom-call | tf_op jit(solution)/shard_map/refine/pallas_call | solution.py:195
  40.2 5.6 %collective-permute-start.2 = (f32[16,64,256]{2,1,0:T(8,128)S(1)}, f32[16,64,256]{2,1,0:T(8,128)}, u32[]{:S(2)}, u32[]{:S(2)}) collective-permute-start(f32[16,64,256]{2,1,0:T(8,128)S(1)} %refine.4.refs_3_), channel_id=1, source_target_pairs={{0,1},{1,2},{2,3},{3,4},{4,5},{5,6},{6,7},{7,8},{8,9},{9,10},{10,1... | collective-permute-start | bytes 3145736 | tf_op jit(solution)/shard_map/ppermute | solution.py:225
  45.8 1.0 copy-done.9
  46.8 12.3 %collective-permute-done.2.refs_2_ = f32[16,64,256]{2,1,0:T(8,128)} collective-permute-done((f32[16,64,256]{2,1,0:T(8,128)S(1)}, f32[16,64,256]{2,1,0:T(8,128)}, u32[]{:S(2)}, u32[]{:S(2)}) %collective-permute-start.2) | collective-permute-done | bytes 1048608 | tf_op jit(solution)/shard_map/ppermute | solution.py:225
  59.2 1.3 collective-permute-start.3
  60.5 0.1 pad_add_fusion.1.refs_0_
  60.6 17.7 %collective-permute-done.3.refs_1_ = f32[16,64,256]{2,1,0:T(8,128)} collective-permute-done((f32[16,64,256]{2,1,0:T(8,128)}, f32[16,64,256]{2,1,0:T(8,128)}, u32[]{:S(2)}, u32[]{:S(2)}) %collective-permute-start.3) | collective-permute-done | bytes 1048608 | tf_op jit(solution)/shard_map/ppermute | solution.py:225
  78.3 1.0 copy-done.2
  79.3 1.2 copy-done.10
  80.5 15.3 %refine.5.refs_3_ = f32[16,64,256]{2,1,0:T(8,128)S(1)} custom-call(s32[3]{0:T(128)S(1)} %pad_add_fusion.1.refs_0_, f32[16,64,256]{2,1,0:T(8,128)} %collective-permute-done.3.refs_1_, f32[16,64,256]{2,1,0:T(8,128)} %collective-permute-done.2.refs_2_, f32[16,64,256]{2,1,0:T(8,128)S(1)} %copy-done.10, bf16[1,4,32,64,256]{4,3,2,1,0:T(8,128)(2,1)} %refs_4_.7, ...), custom_call_target="tpu_custom_call" | custom-call | tf_op jit(solution)/shard_map/refine/pallas_call | solution.py:195
  95.8 0.1 collective-permute-start.4
  95.9 0.0 copy-start.7
  95.9 1.0 copy-done.7
  96.9 16.0 %collective-permute-done.4.refs_2_ = f32[16,64,256]{2,1,0:T(8,128)} collective-permute-done((f32[16,64,256]{2,1,0:T(8,128)S(1)}, f32[16,64,256]{2,1,0:T(8,128)}, u32[]{:S(2)}, u32[]{:S(2)}) %collective-permute-start.4) | collective-permute-done | bytes 1048608 | tf_op jit(solution)/shard_map/ppermute | solution.py:225
  112.9 1.9 collective-permute-start.5
  114.8 0.1 pad_add_fusion.2.refs_0_
  114.9 17.1 %collective-permute-done.5.refs_1_ = f32[16,64,256]{2,1,0:T(8,128)} collective-permute-done((f32[16,64,256]{2,1,0:T(8,128)}, f32[16,64,256]{2,1,0:T(8,128)}, u32[]{:S(2)}, u32[]{:S(2)}) %collective-permute-start.5) | collective-permute-done | bytes 1048608 | tf_op jit(solution)/shard_map/ppermute | solution.py:225
  132.0 1.0 copy-done.3
  133.0 1.2 copy-done.8
  134.3 15.3 %refine.6.refs_3_ = f32[16,64,256]{2,1,0:T(8,128)S(1)} custom-call(s32[3]{0:T(128)S(1)} %pad_add_fusion.2.refs_0_, f32[16,64,256]{2,1,0:T(8,128)} %collective-permute-done.5.refs_1_, f32[16,64,256]{2,1,0:T(8,128)} %collective-permute-done.4.refs_2_, f32[16,64,256]{2,1,0:T(8,128)S(1)} %copy-done.8, bf16[1,4,32,64,256]{4,3,2,1,0:T(8,128)(2,1)} %refs_4_.7, ...), custom_call_target="tpu_custom_call" | custom-call | tf_op jit(solution)/shard_map/refine/pallas_call | solution.py:195
  149.6 0.1 collective-permute-start.6
  149.7 1.0 copy-done.5
  150.6 16.0 %collective-permute-done.6.refs_2_ = f32[16,64,256]{2,1,0:T(8,128)} collective-permute-done((f32[16,64,256]{2,1,0:T(8,128)S(1)}, f32[16,64,256]{2,1,0:T(8,128)}, u32[]{:S(2)}, u32[]{:S(2)}) %collective-permute-start.6) | collective-permute-done | bytes 1048608 | tf_op jit(solution)/shard_map/ppermute | solution.py:225
  166.7 1.9 collective-permute-start.7
  168.6 0.1 pad_add_fusion.3.refs_0_
  168.7 17.1 %collective-permute-done.7.refs_1_ = f32[16,64,256]{2,1,0:T(8,128)} collective-permute-done((f32[16,64,256]{2,1,0:T(8,128)}, f32[16,64,256]{2,1,0:T(8,128)}, u32[]{:S(2)}, u32[]{:S(2)}) %collective-permute-start.7) | collective-permute-done | bytes 1048608 | tf_op jit(solution)/shard_map/ppermute | solution.py:225
  185.8 1.0 copy-done.4
  186.8 1.2 copy-done.6
  188.0 15.3 %refine.7 = f32[16,64,256]{2,1,0:T(8,128)S(1)} custom-call(s32[3]{0:T(128)S(1)} %pad_add_fusion.3.refs_0_, f32[16,64,256]{2,1,0:T(8,128)} %collective-permute-done.7.refs_1_, f32[16,64,256]{2,1,0:T(8,128)} %collective-permute-done.6.refs_2_, f32[16,64,256]{2,1,0:T(8,128)S(1)} %copy-done.6, bf16[1,4,32,64,256]{4,3,2,1,0:T(8,128)(2,1)} %refs_4_.7, ...), custom_call_target="tpu_custom_call" | custom-call | tf_op jit(solution)/shard_map/refine/pallas_call | solution.py:195
  203.3 0.1 collective-permute-start.8
  203.4 14.9 %collective-permute-done.8 = f32[16,64,256]{2,1,0:T(8,128)S(1)} collective-permute-done((f32[16,64,256]{2,1,0:T(8,128)S(1)}, f32[16,64,256]{2,1,0:T(8,128)S(1)}, u32[]{:S(2)}, u32[]{:S(2)}) %collective-permute-start.8) | collective-permute-done | bytes 1048608 | tf_op jit(solution)/shard_map/ppermute | solution.py:225
  218.3 1.0 copy.30
  (14 shorter events, 0.0 us)
Async XLA Ops:
  0.0 22.7 %collective-permute-start = (f32[16,64,256]{2,1,0:T(8,128)}, f32[16,64,256]{2,1,0:T(8,128)}, u32[]{:S(2)}, u32[]{:S(2)}) collective-permute-start(f32[16,64,256]{2,1,0:T(8,128)} %refs_2_.1), channel_id=1, source_target_pairs={{0,1},{1,2},{2,3},{3,4},{4,5},{5,6},{6,7},{7,8},{8,9},{9,10},{10,1... | collective-permute-start | bytes 3145736 | tf_op jit(solution)/shard_map/ppermute | solution.py:225
  3.3 19.3 %collective-permute-start.1 = (f32[16,64,256]{2,1,0:T(8,128)}, f32[16,64,256]{2,1,0:T(8,128)}, u32[]{:S(2)}, u32[]{:S(2)}) collective-permute-start(f32[16,64,256]{2,1,0:T(8,128)} %refs_2_.1), channel_id=1, source_target_pairs={{1,0},{2,1},{3,2},{4,3},{5,4},{6,5},{7,6},{8,7},{9,8},{10,9},{11,1... | collective-permute-start | bytes 3145736 | tf_op jit(solution)/shard_map/ppermute | solution.py:225
  21.9 0.7 copy-start
  22.7 1.0 copy-start.1
  23.7 1.2 copy-start.11
  40.2 19.0 %collective-permute-start.2 = (f32[16,64,256]{2,1,0:T(8,128)S(1)}, f32[16,64,256]{2,1,0:T(8,128)}, u32[]{:S(2)}, u32[]{:S(2)}) collective-permute-start(f32[16,64,256]{2,1,0:T(8,128)S(1)} %refine.4.refs_3_), channel_id=1, source_target_pairs={{0,1},{1,2},{2,3},{3,4},{4,5},{5,6},{6,7},{7,8},{8,9},{9,10},{10,1... | collective-permute-start | bytes 3145736 | tf_op jit(solution)/shard_map/ppermute | solution.py:225
  45.8 1.0 copy-start.9
  59.2 19.1 %collective-permute-start.3 = (f32[16,64,256]{2,1,0:T(8,128)}, f32[16,64,256]{2,1,0:T(8,128)}, u32[]{:S(2)}, u32[]{:S(2)}) collective-permute-start(f32[16,64,256]{2,1,0:T(8,128)} %collective-permute-done.2.refs_2_), channel_id=1, source_target_pairs={{1,2},{2,3},{3,4},{4,5},{5,6},{6,7},{7,8},{8,9},{9,10},{10,11},{11... | collective-permute-start | bytes 3145736 | tf_op jit(solution)/shard_map/ppermute | solution.py:225
  78.3 1.0 copy-start.2
  79.3 1.2 copy-start.10
  95.8 17.1 %collective-permute-start.4 = (f32[16,64,256]{2,1,0:T(8,128)S(1)}, f32[16,64,256]{2,1,0:T(8,128)}, u32[]{:S(2)}, u32[]{:S(2)}) collective-permute-start(f32[16,64,256]{2,1,0:T(8,128)S(1)} %refine.5.refs_3_), channel_id=1, source_target_pairs={{0,1},{1,2},{2,3},{3,4},{4,5},{5,6},{6,7},{7,8},{8,9},{9,10},{10,1... | collective-permute-start | bytes 3145736 | tf_op jit(solution)/shard_map/ppermute | solution.py:225
  95.9 1.0 copy-start.7
  112.9 19.1 %collective-permute-start.5 = (f32[16,64,256]{2,1,0:T(8,128)}, f32[16,64,256]{2,1,0:T(8,128)}, u32[]{:S(2)}, u32[]{:S(2)}) collective-permute-start(f32[16,64,256]{2,1,0:T(8,128)} %collective-permute-done.4.refs_2_), channel_id=1, source_target_pairs={{0,1},{2,3},{3,4},{4,5},{5,6},{6,7},{7,8},{8,9},{9,10},{10,11},{11... | collective-permute-start | bytes 3145736 | tf_op jit(solution)/shard_map/ppermute | solution.py:225
  132.0 1.0 copy-start.3
  133.0 1.2 copy-start.8
  149.6 17.1 %collective-permute-start.6 = (f32[16,64,256]{2,1,0:T(8,128)S(1)}, f32[16,64,256]{2,1,0:T(8,128)}, u32[]{:S(2)}, u32[]{:S(2)}) collective-permute-start(f32[16,64,256]{2,1,0:T(8,128)S(1)} %refine.6.refs_3_), channel_id=1, source_target_pairs={{0,1},{1,2},{2,3},{3,4},{4,5},{5,6},{6,7},{7,8},{8,9},{9,10},{10,1... | collective-permute-start | bytes 3145736 | tf_op jit(solution)/shard_map/ppermute | solution.py:225
  149.7 1.0 copy-start.5
  166.7 19.1 %collective-permute-start.7 = (f32[16,64,256]{2,1,0:T(8,128)}, f32[16,64,256]{2,1,0:T(8,128)}, u32[]{:S(2)}, u32[]{:S(2)}) collective-permute-start(f32[16,64,256]{2,1,0:T(8,128)} %collective-permute-done.6.refs_2_), channel_id=1, source_target_pairs={{0,1},{1,2},{3,4},{4,5},{5,6},{6,7},{7,8},{8,9},{9,10},{10,11},{11... | collective-permute-start | bytes 3145736 | tf_op jit(solution)/shard_map/ppermute | solution.py:225
  185.8 1.0 copy-start.4
  186.8 1.2 copy-start.6
  203.3 14.9 %collective-permute-start.8 = (f32[16,64,256]{2,1,0:T(8,128)S(1)}, f32[16,64,256]{2,1,0:T(8,128)S(1)}, u32[]{:S(2)}, u32[]{:S(2)}) collective-permute-start(f32[16,64,256]{2,1,0:T(8,128)S(1)} %refine.7), channel_id=1, source_target_pairs={{0,13},{1,14},{2,15},{3,0},{4,1},{5,2},{6,3},{7,4},{8,5},{9,6},{10... | collective-permute-start | bytes 3145736 | tf_op jit(solution)/shard_map/ppermute | solution.py:225
